TPU v7x, 32 devices: a whole 2x2x4 slice. The times are simulated.
32 devices in a mesh: tm: 8 (over z, y), mel: 4 (over x, core).
Axes of the slice: x: 2, y: 2, z: 4, core: 2. Of those that a mesh axis runs over, the one named last changes fastest.
Arguments:
- act_one: bfloat16 [1024, 16384], P('tm', 'mel'), may hold values from -6 to 6
- act_two: bfloat16 [1024, 16384], P('tm', 'mel'), may hold values from -6 to 6
- act_three: bfloat16 [512, 16384], P('tm', 'mel'), may hold values from -6 to 6
- act_four: bfloat16 [512, 16384], P('tm', 'mel'), may hold values from -6 to 6
- target_one: bfloat16 [512, 8192], P('tm', 'mel'), may hold values from -6 to 6
- target_two: bfloat16 [256, 8192], P('tm', 'mel'), may hold values from -6 to 6
- kernel_one: bfloat16 [3, 3, 1, 64], replicated, may hold values from -2 to 2
- kernel_two: bfloat16 [3, 3, 64, 64], replicated, may hold values from -0.25 to 0.25
- kernel_three: bfloat16 [3, 3, 64, 128], replicated, may hold values from -0.25 to 0.25
- kernel_four: bfloat16 [3, 3, 128, 128], replicated, may hold values from -0.1875 to 0.1875
- mel_power: float32 [1024, 256], P('tm', 'mel'), may hold values from 0.05 to 20
- loudness: float32 [256], P('mel'), may hold values from 0.1 to 10
- filters: float32 [512, 256], replicated, may hold values from -0.375 to 0.375
- spec_real: float32 [1024, 512], P('tm', 'mel'), may hold values from -6 to 6
- spec_imag: float32 [1024, 512], P('tm', 'mel'), may hold values from -6 to 6
Outputs:
- wave_grad: float32 [524288], P(('tm', 'mel'))
All inputs are finite; a program needn't handle non-finite values.
Results may differ from a plain program's by a relative error of at most 0.015.
Values may be sent and summed in bfloat16 or wider, within the bound.
A program may use at most 64 MiB of HBM per device.

v0:
```python
import functools

import jax
import jax.numpy as jnp
import ml_dtypes
import numpy as np
from jax import lax
from jax.experimental import pallas as pl
from jax.experimental.pallas import tpu as pltpu
from jax.sharding import PartitionSpec as P

LANES = 128
TILE = 16
SIDE = 4
EDGE = SIDE * LANES
MESH = pl.DeviceIdType.MESH
BF16 = jnp.bfloat16
F32 = jnp.float32

DEPTH = (1, 2, 2, 4, 1, 2)
PLACE = (0, 1, 3, 5, 9, 10)
WIDTH = (128, 128, 256, 512, 128, 256)


def synthesis_table(bins):
    points = 2 * bins
    sample = np.arange(points)
    angle = (np.arange(bins)[:, None] * sample[None, :] % points) * (2.0 * np.pi / points)
    window = 0.5 - 0.5 * np.cos(sample * (2.0 * np.pi / points))
    scale = 2.0 * window * points**-0.5
    table = np.concatenate([np.cos(angle) * scale, -np.sin(angle) * scale], axis=0)
    return table.astype(np.float32).astype(ml_dtypes.bfloat16)


def iota2(rows, cols):
    return (
        lax.broadcasted_iota(jnp.int32, (rows, cols), 0),
        lax.broadcasted_iota(jnp.int32, (rows, cols), 1),
    )


def as_bf16(mask, value=1.0):
    return jnp.where(mask, value, 0.0).astype(F32).astype(BF16)


def coarser(row, main):
    return row // 2 + jnp.where(row >= main + TILE // 2, TILE // 2, 0)


def dot(a, b):
    return jnp.dot(a, b, preferred_element_type=F32)


def dot_nt(a, b):
    return lax.dot_general(a, b, (((1,), (1,)), ((), ())), preferred_element_type=F32)


def kernel(
    n_tm,
    n_mel,
    act_one,
    act_two,
    act_three,
    act_four,
    target_one,
    target_two,
    filters,
    table,
    kernel_one,
    kernel_two,
    kernel_three,
    kernel_four,
    mel_power,
    loudness,
    spec_real,
    spec_imag,
    out,
    e1,
    e2,
    e3,
    e4,
    t1,
    t2,
    filters_v,
    table_v,
    pack,
    rows_in,
    ga,
    gb,
    gc,
    gd,
    w4,
    w3,
    w2,
    wb,
    spec_out,
    spec_in,
    mel_out,
    mel_in,
    load_sem,
    halo_send,
    halo_recv,
    spec_send,
    spec_recv,
    mel_send,
    mel_recv,
):
    tm, mel = lax.axis_index("tm"), lax.axis_index("mel")
    length = act_one.shape[1]
    inputs = (act_one, act_two, act_three, act_four, target_one, target_two)
    wide = (e1, e2, e3, e4, t1, t2)
    frames, coarse = act_one.shape[0], act_three.shape[0]
    fine_rows, coarse_rows = e1.shape[0], e3.shape[0]
    tiles = e1.shape[1] // LANES
    share = frames // n_mel

    loads = []
    for at, (src, dst) in enumerate(zip(inputs, wide)):
        rows, cols = src.shape
        loads.append(
            pltpu.make_async_copy(
                src, dst.at[pl.ds(0, rows), pl.ds(EDGE, cols)], load_sem.at[at]
            )
        )
    loads.append(pltpu.make_async_copy(filters, filters_v, load_sem.at[6]))
    loads.append(pltpu.make_async_copy(table, table_v, load_sem.at[7]))
    for load in loads:
        load.start()

    for src, dst in zip(inputs, wide):
        rows, cols = src.shape
        dst[pl.ds(0, rows), pl.ds(0, EDGE)] = jnp.zeros((rows, EDGE), BF16)
        dst[pl.ds(0, rows), pl.ds(EDGE + cols, EDGE)] = jnp.zeros((rows, EDGE), BF16)
    rows_in[...] = jnp.zeros(rows_in.shape, BF16)
    spec_in[...] = jnp.zeros(spec_in.shape, BF16)
    mel_in[...] = jnp.zeros(mel_in.shape, BF16)

    barrier = pltpu.get_barrier_semaphore()

    def has(dt, dm):
        cond = jnp.bool_(True)
        if dt:
            cond = (tm > 0) if dt < 0 else (tm < n_tm - 1)
        if dm:
            side = (mel > 0) if dm < 0 else (mel < n_mel - 1)
            cond = side if not dt else jnp.logical_and(cond, side)
        return cond

    for dt in (-1, 0, 1):
        for k in range(n_mel):
            if dt == 0 and k == 0:
                continue

            def greet(dt=dt, k=k):
                pl.semaphore_signal(
                    barrier,
                    inc=1,
                    device_id={"tm": tm + dt, "mel": lax.rem(mel + k, n_mel)},
                    device_id_type=MESH,
                )

            if dt:
                pl.when(has(dt, 0))(greet)
            else:
                greet()
    rows_of_peers = 1 + jnp.where(tm > 0, 1, 0) + jnp.where(tm < n_tm - 1, 1, 0)
    pl.semaphore_wait(barrier, n_mel * rows_of_peers - 1)

    halo = []

    def add_halo(dt, dm, src, dst):
        at = len(halo)
        copy = pltpu.make_async_remote_copy(
            src_ref=src,
            dst_ref=dst,
            send_sem=halo_send.at[at],
            recv_sem=halo_recv.at[at],
            device_id={"tm": tm + dt, "mel": mel + dm},
            device_id_type=MESH,
        )
        halo.append((dt, dm, copy))
        pl.when(has(dt, dm))(copy.start)

    for src, dst, width in zip(inputs, wide, WIDTH):
        rows, cols = src.shape
        add_halo(
            0,
            1,
            src.at[:, pl.ds(cols - width, width)],
            dst.at[pl.ds(0, rows), pl.ds(EDGE - width, width)],
        )
        add_halo(
            0,
            -1,
            src.at[:, pl.ds(0, width)],
            dst.at[pl.ds(0, rows), pl.ds(EDGE + cols, width)],
        )

    def exchange(src, dst, send, recv):
        copies = []
        for k in range(n_mel):
            j = lax.rem(mel + k, n_mel)
            main = pl.ds(pl.multiple_of(j * share, TILE), share)
            before = pl.ds(
                pl.multiple_of(lax.rem(j * share + frames - TILE, frames), TILE), TILE
            )
            if k:
                copy = pltpu.make_async_remote_copy(
                    src_ref=src.at[main],
                    dst_ref=dst.at[mel, pl.ds(0, share)],
                    send_sem=send.at[k],
                    recv_sem=recv.at[k],
                    device_id={"tm": tm, "mel": j},
                    device_id_type=MESH,
                )
                copy.start()
                copies.append((copy, None, None))
            copy = pltpu.make_async_remote_copy(
                src_ref=src.at[before],
                dst_ref=dst.at[mel, pl.ds(share, TILE)],
                send_sem=send.at[n_mel + k],
                recv_sem=recv.at[n_mel + k],
                device_id={"tm": tm + jnp.where(j == 0, 1, 0), "mel": j},
                device_id_type=MESH,
            )
            if k:
                sends = jnp.logical_or(j > 0, tm < n_tm - 1)
                receives = jnp.logical_or(mel > 0, tm > 0)
            else:
                sends = jnp.logical_and(mel == 0, tm < n_tm - 1)
                receives = jnp.logical_and(mel == 0, tm > 0)
            pl.when(sends)(copy.start)
            copies.append((copy, sends, receives))
        dst[mel, pl.ds(0, share)] = src[pl.ds(pl.multiple_of(mel * share, TILE), share)]

        @pl.when(mel > 0)
        def _():
            dst[mel, pl.ds(share, TILE)] = src[
                pl.ds(pl.multiple_of(mel * share - TILE, TILE), TILE)
            ]

        return copies

    def finish(copies):
        for copy, sends, receives in copies:
            if sends is None:
                copy.wait_recv()
            else:
                pl.when(receives)(copy.wait_recv)
        for copy, sends, receives in copies:
            if sends is None:
                copy.wait_send()
            else:
                pl.when(sends)(copy.wait_send)

    spec_out[:, pl.ds(0, spec_real.shape[1])] = spec_real[...].astype(BF16)
    spec_out[:, pl.ds(spec_real.shape[1], spec_imag.shape[1])] = spec_imag[...].astype(BF16)

    for load in loads[:6]:
        load.wait()
    o, c = iota2(TILE, 6 * TILE)
    first_rows = jnp.zeros((TILE, 6 * TILE), jnp.bool_)
    last_rows = jnp.zeros((TILE, 6 * TILE), jnp.bool_)
    for x in range(6):
        inside = (o >= PLACE[x]) & (o < PLACE[x] + DEPTH[x])
        first_rows |= inside & (c - x * TILE == o - PLACE[x])
        last_rows |= inside & (c - x * TILE - (TILE - DEPTH[x]) == o - PLACE[x])
    picks = (as_bf16(first_rows), as_bf16(last_rows))
    target_length = target_one.shape[1]
    for chunk in range(length // EDGE):
        for end in (0, 1):
            parts = []
            for x, (src, dst) in enumerate(zip(inputs, wide)):
                lane = EDGE + (chunk * EDGE) % (target_length if x >= 4 else length)
                row = src.shape[0] - TILE if end else 0
                parts.append(dst[pl.ds(row, TILE), pl.ds(lane, EDGE)])
            pack[end, :, pl.ds(chunk * EDGE, EDGE)] = dot(
                picks[end], jnp.concatenate(parts, axis=0)
            ).astype(BF16)
    for end, dt in ((1, 1), (0, -1)):
        at = 1 - end
        add_halo(dt, 0, pack.at[end], rows_in.at[at, :, pl.ds(EDGE, length)])
        add_halo(
            dt, 1, pack.at[end, :, pl.ds(length - EDGE, EDGE)], rows_in.at[at, :, pl.ds(0, EDGE)]
        )
        add_halo(
            dt, -1, pack.at[end, :, pl.ds(0, EDGE)], rows_in.at[at, :, pl.ds(EDGE + length, EDGE)]
        )
    spec_copies = exchange(spec_out, spec_in, spec_send, spec_recv)

    w4[...] = jnp.zeros(w4.shape, BF16)
    w3[...] = jnp.zeros(w3.shape, BF16)
    half = LANES // 2
    blank = jnp.zeros((half, half), F32)
    for i in range(3):
        for k in range(4):
            lanes = pl.ds((i * 4 + k) * LANES, LANES)
            for n in range(2):
                j = n - (k - 1)
                if abs(j) <= 1:
                    w4[pl.ds(n * LANES, LANES), lanes] = kernel_four[i, j + 1]
                    w3[pl.ds(n * LANES, half), lanes] = kernel_three[i, j + 1]
                    w3[pl.ds(n * LANES + half, half), lanes] = kernel_three[i, j + 1]
                for a in range(2):
                    pair = []
                    for b in range(2):
                        j = (2 * n + a) - (2 * (k - 1) + b)
                        pair.append(
                            kernel_two[i, j + 1].astype(F32) if abs(j) <= 1 else blank
                        )
                    w2[pl.ds(n * LANES + a * half, half), lanes] = jnp.concatenate(
                        pair, axis=1
                    ).astype(BF16)
    mels = mel_power.shape[1]
    one = kernel_one[...].astype(F32)
    one = jnp.concatenate([one, one], axis=1)
    m, lane = iota2(mels, LANES)

    def band(s, carry):
        d = m - (2 * (s - SIDE) + lane // half)
        for i in range(3):
            value = jnp.zeros((mels, LANES), F32)
            for j in range(3):
                value = jnp.where(d == j - 1, one[3 * i + j][None, :], value)
            wb[s, pl.ds(i * mels, mels)] = value.astype(BF16)
        wb[s, pl.ds(3 * mels, mels)] = jnp.zeros((mels, LANES), BF16)
        return carry

    lax.fori_loop(2, tiles - 2, band, 0)
    for g in (gb, gc):
        for s in (1, tiles - 2):
            for i in range(3):
                g[i, s] = jnp.zeros(g.shape[2:], BF16)

    for dt, dm, copy in halo:
        pl.when(has(-dt, -dm))(copy.wait_recv)
    o, c = iota2(6 * TILE, 2 * TILE)
    spots = jnp.zeros((6 * TILE, 2 * TILE), jnp.bool_)
    for x in range(6):
        for at, base in ((0, TILE - DEPTH[x]), (1, 0)):
            r, p = o - x * TILE - base, c - at * TILE - PLACE[x]
            spots |= (r == p) & (r >= 0) & (r < DEPTH[x])
    spots = as_bf16(spots)
    chunks = (length + 2 * EDGE) // EDGE
    target_chunks = target_length // EDGE
    for chunk in range(chunks):
        lanes = pl.ds(chunk * EDGE, EDGE)
        both = jnp.concatenate([rows_in[0, :, lanes], rows_in[1, :, lanes]], axis=0)
        placed = dot(spots, both).astype(BF16)
        for x, (src, dst) in enumerate(zip(inputs, wide)):
            at = lanes
            if x >= 4:
                if chunk == chunks - 1:
                    at = pl.ds((target_chunks + 1) * EDGE, EDGE)
                elif chunk > target_chunks:
                    continue
            dst[pl.ds(src.shape[0], TILE), at] = placed[x * TILE : (x + 1) * TILE]

    def shifted(g, s, value):
        rows = value.shape[0]
        g[0, s] = pltpu.roll(value, rows - 1, 0).astype(BF16)
        g[1, s] = value.astype(BF16)
        g[2, s] = pltpu.roll(value, 1, 0).astype(BF16)

    def tile_at(s, count=1):
        return pl.ds(pl.multiple_of(s * LANES, LANES), count * LANES)

    r, s_ = iota2(coarse_rows, coarse_rows)
    mean_rows = as_bf16(r // 2 == s_ // 2, 0.25)
    r, s_ = iota2(coarse_rows, t2.shape[0])
    spread_two = as_bf16(coarser(r, coarse) == s_)

    def top(p, carry):
        x = e4[:, tile_at(2 * p, 2)].astype(F32)
        means = dot(mean_rows, jnp.maximum(x, 0.0).astype(BF16))
        wanted = dot(spread_two, t2[:, tile_at(p + SIDE // 2)])
        diff = 0.25 * (means[:, :LANES] + means[:, LANES:] - wanted)
        for n in range(2):
            shifted(ga, 2 * p + n, jnp.where(x[:, n * LANES : (n + 1) * LANES] > 0, diff, 0.0))
        return carry

    lax.fori_loop(0, tiles // 2, top, 0)

    def conv(g, weights, group, epilogue):
        rows = g.shape[2]
        pairs = (tiles - 4) // 2

        def step(q, carry):
            base = 2 + 2 * group * q
            lhs = jnp.concatenate(
                [
                    jnp.concatenate(
                        [g[i, base + 2 * u - 1 + k] for i in range(3) for k in range(4)], axis=1
                    )
                    for u in range(group)
                ],
                axis=0,
            )
            result = dot_nt(lhs, weights[...])
            for u in range(group):
                epilogue(base + 2 * u, result[u * rows : (u + 1) * rows])
            return carry

        lax.fori_loop(0, pairs // group, step, 0)

    def third(s, value):
        x = e3[:, tile_at(s, 2)].astype(F32)
        masked = jnp.where(x > 0, value, 0.0)
        for n in range(2):
            shifted(gb, s + n, masked[:, n * LANES : (n + 1) * LANES])

    conv(ga, w4, 6, third)

    r, s_ = iota2(coarse_rows, fine_rows)
    pool_rows = as_bf16(coarser(s_, frames) == r, 0.25)
    r, s_ = iota2(fine_rows, coarse_rows)
    spread_rows = as_bf16(coarser(r, frames) == s_)
    low = lax.broadcasted_iota(jnp.int32, (coarse_rows, LANES), 1) < half

    def second(s, value):
        x = e2[:, tile_at(s, 2)].astype(F32)
        sums = dot(pool_rows, jnp.maximum(x, 0.0).astype(BF16))
        want = t1[:, tile_at((s - SIDE) // 2 + SIDE)].astype(F32)
        turned = pltpu.roll(want, half, 1)
        wants = (jnp.where(low, want, turned), jnp.where(low, turned, want))
        parts = []
        for n in range(2):
            lanes = slice(n * LANES, (n + 1) * LANES)
            feat = sums[:, lanes] + pltpu.roll(sums[:, lanes], half, 1)
            parts.append((0.25 * (value[:, lanes] + feat - wants[n])).astype(BF16))
        fine = dot(spread_rows, jnp.concatenate(parts, axis=1))
        masked = jnp.where(x > 0, fine, 0.0)
        for n in range(2):
            shifted(gc, s + n, masked[:, n * LANES : (n + 1) * LANES])

    conv(gb, w3, 6, second)

    def first(s, value):
        x = e1[:, tile_at(s, 2)].astype(F32)
        masked = jnp.where(x > 0, value, 0.0).astype(BF16)
        for n in range(2):
            gd[s + n] = masked[:, n * LANES : (n + 1) * LANES]

    conv(gc, w2, 3, first)

    total = jnp.zeros((fine_rows, 4 * mels), F32)
    for s in range(2, tiles - 2, 2):
        total += dot_nt(
            jnp.concatenate([gd[s], gd[s + 1]], axis=1),
            jnp.concatenate([wb[s], wb[s + 1]], axis=1),
        )
    left, right = total[:, : 2 * mels], total[:, 2 * mels :]
    grad_log = (
        pltpu.roll(left, fine_rows - 1, 0) + pltpu.roll(left, mels, 1) + pltpu.roll(right, 1, 0)
    )[:frames, :mels]
    loud = loudness[...]
    grad_mel = grad_log * loud / (1.0 + loud * mel_power[...])
    twice = jnp.concatenate([grad_mel, grad_mel], axis=1)
    lane = lax.broadcasted_iota(jnp.int32, twice.shape, 1)
    mel_out[...] = jnp.where(lane // mels == lax.rem(mel, 2), twice, 0.0).astype(BF16)
    mel_copies = exchange(mel_out, mel_in, mel_send, mel_recv)

    for dt, dm, copy in halo:
        pl.when(has(dt, dm))(copy.wait_send)
    finish(spec_copies)
    loads[6].wait()
    loads[7].wait()
    finish(mel_copies)

    whole = jnp.concatenate(
        [mel_in[2 * a] + mel_in[2 * a + 1] for a in range(n_mel // 2)], axis=1
    )
    power = dot_nt(whole, filters_v[...].astype(BF16))
    per = spec_real.shape[1]
    grads = []
    for part in range(2):
        for j in range(n_mel):
            spec = spec_in[j, :, pl.ds(part * per, per)].astype(F32)
            grads.append((power[:, j * per : (j + 1) * per] * spec).astype(BF16))
    made = dot(jnp.concatenate(grads, axis=1), table_v[...])
    hop = made.shape[1] // 2
    blocks = made[:, :hop] + pltpu.roll(made[:, hop:], 1, 0)
    for a in range(hop // LANES):
        out[pl.ds(a, share, stride=hop // LANES), :] = blocks[
            :share, a * LANES : (a + 1) * LANES
        ]


def shards(
    act_one,
    act_two,
    act_three,
    act_four,
    target_one,
    target_two,
    kernel_one,
    kernel_two,
    kernel_three,
    kernel_four,
    mel_power,
    loudness,
    filters,
    spec_real,
    spec_imag,
):
    n_tm, n_mel = lax.axis_size("tm"), lax.axis_size("mel")
    frames, mels = mel_power.shape
    bins = filters.shape[0]
    table = jnp.asarray(synthesis_table(bins))
    share = frames // n_mel
    ext = lambda a: pltpu.VMEM((a.shape[0] + TILE, a.shape[1] + 2 * EDGE), BF16)
    length = act_one.shape[1]
    tiles = (length + 2 * EDGE) // LANES
    fine_rows, coarse_rows = frames + TILE, frames // 2 + TILE
    any_spec = pl.BlockSpec(memory_space=pl.ANY)
    vmem = pl.BlockSpec(memory_space=pltpu.VMEM)
    result = pl.pallas_call(
        functools.partial(kernel, n_tm, n_mel),
        out_shape=jax.ShapeDtypeStruct((share * bins // LANES, LANES), F32),
        in_specs=[any_spec] * 8 + [vmem] * 8,
        out_specs=vmem,
        scratch_shapes=[
            ext(act_one),
            ext(act_two),
            ext(act_three),
            ext(act_four),
            ext(target_one),
            ext(target_two),
            pltpu.VMEM(filters.shape, F32),
            pltpu.VMEM(table.shape, BF16),
            pltpu.VMEM((2, TILE, length), BF16),
            pltpu.VMEM((2, TILE, length + 2 * EDGE), BF16),
            pltpu.VMEM((3, tiles, coarse_rows, LANES), BF16),
            pltpu.VMEM((3, tiles, coarse_rows, LANES), BF16),
            pltpu.VMEM((3, tiles, fine_rows, LANES), BF16),
            pltpu.VMEM((tiles, fine_rows, LANES), BF16),
            pltpu.VMEM((2 * LANES, 12 * LANES), BF16),
            pltpu.VMEM((2 * LANES, 12 * LANES), BF16),
            pltpu.VMEM((2 * LANES, 12 * LANES), BF16),
            pltpu.VMEM((tiles, 4 * mels, LANES), BF16),
            pltpu.VMEM((frames, 2 * spec_real.shape[1]), BF16),
            pltpu.VMEM((n_mel, share + TILE, 2 * spec_real.shape[1]), BF16),
            pltpu.VMEM((frames, 2 * mels), BF16),
            pltpu.VMEM((n_mel, share + TILE, 2 * mels), BF16),
            pltpu.SemaphoreType.DMA((8,)),
            pltpu.SemaphoreType.DMA((18,)),
            pltpu.SemaphoreType.DMA((18,)),
            pltpu.SemaphoreType.DMA((2 * n_mel,)),
            pltpu.SemaphoreType.DMA((2 * n_mel,)),
            pltpu.SemaphoreType.DMA((2 * n_mel,)),
            pltpu.SemaphoreType.DMA((2 * n_mel,)),
        ],
        compiler_params=pltpu.CompilerParams(
            collective_id=0, has_side_effects=True, vmem_limit_bytes=56 * 2**20
        ),
        name="wave_gradient",
    )(
        act_one,
        act_two,
        act_three,
        act_four,
        target_one,
        target_two,
        filters,
        table,
        kernel_one.reshape(9, kernel_one.shape[3]),
        kernel_two,
        kernel_three,
        kernel_four,
        mel_power,
        loudness.reshape(1, mels),
        spec_real,
        spec_imag,
    )
    return result.reshape(-1)


def solution(mesh):
    return jax.shard_map(
        shards,
        mesh=mesh,
        in_specs=(
            P("tm", "mel"),
            P("tm", "mel"),
            P("tm", "mel"),
            P("tm", "mel"),
            P("tm", "mel"),
            P("tm", "mel"),
            P(),
            P(),
            P(),
            P(),
            P("tm", "mel"),
            P("mel"),
            P(),
            P("tm", "mel"),
            P("tm", "mel"),
        ),
        out_specs=P(("tm", "mel")),
        check_vma=False,
    )
```

profile of v0, /device:TPU:25, one launch (start us, length us, event | category | flops | bytes accessed | tf_op | source)
XLA Modules:
  0.0 38.5 jit_solution(2226451805552823567)
XLA Ops:
  0.0 1.3 %reshape.9.kernel_one = bf16[9,64]{1,0:T(8,128)(2,1)} reshape(bf16[3,3,1,64]{3,1,2,0:T(4,128)(2,1)} %param.22) | data formatting | bytes 2304 | tf_op jit(solution)/shard_map/reshape | solution.py:566
  1.3 1.5 %copy.17.mel_power = f32[128,64]{1,0:T(8,128)} copy(f32[128,64]{0,1:T(8,128)} %param.26) | data formatting | bytes 65536 | tf_op args[10]
  2.8 34.3 %wave_gradient.1 = f32[128,128]{1,0:T(8,128)} custom-call(bf16[128,4096]{1,0:T(8,128)(2,1)} %act_one.1, bf16[128,4096]{1,0:T(8,128)(2,1)} %act_two.1, bf16[64,4096]{1,0:T(8,128)(2,1)} %act_three.1, bf16[64,4096]{1,0:T(8,128)(2,1)} %act_four.1, bf16[64,2048]{1,0:T(8,128)(2,1)} %target_one.1, bf16[32,2048]{1,0:T(8,128)(2,1)} %target_two.1, ...), custom_call_target="tpu_custom_call" | custom-call | tf_op jit(solution)/shard_map/wave_gradient/pallas_call | solution.py:517
  37.1 1.5 %copy.19 = f32[16384]{0:T(1024)} copy(f32[16384]{0:T(1024)} %bitcast.4) | data formatting | bytes 131072
where the time goes:
time: 39.2 us; the launch traced here: 38.5 us
  Pallas kernels  34.3 us (87%)
  local copies, waits for them, and re-layouts  4.25 us (11%)
    pallas_call x1, Pallas kernels, shards(): pl.pallas_call(functools.partial(kernel, n_tm, n_mel), out_shape=jax.Shap...  34.3 us
    unnamed x2, local copies, waits for them, and re-layouts  2.96 us
    reshape x1, local copies, waits for them, and re-layouts, shards(): kernel_one.reshape(9, kernel_one.shape[3])  1.29 us

commit v1 on v0

--- a/solution.py
+++ b/solution.py
@@ -89,6 +89,15 @@
     gb,
     gc,
     gd,
+    pre,
+    gain,
+    filters_b,
+    k2_v,
+    k3_v,
+    k4_v,
+    power_v,
+    real_v,
+    imag_v,
     w4,
     w3,
     w2,
@@ -122,8 +131,17 @@
                 src, dst.at[pl.ds(0, rows), pl.ds(EDGE, cols)], load_sem.at[at]
             )
         )
-    loads.append(pltpu.make_async_copy(filters, filters_v, load_sem.at[6]))
-    loads.append(pltpu.make_async_copy(table, table_v, load_sem.at[7]))
+    for src, dst in (
+        (kernel_two, k2_v),
+        (kernel_three, k3_v),
+        (kernel_four, k4_v),
+        (mel_power, power_v),
+        (spec_real, real_v),
+        (spec_imag, imag_v),
+        (filters, filters_v),
+        (table, table_v),
+    ):
+        loads.append(pltpu.make_async_copy(src, dst, load_sem.at[len(loads)]))
     for load in loads:
         load.start()
 
@@ -163,8 +181,6 @@
                 pl.when(has(dt, 0))(greet)
             else:
                 greet()
-    rows_of_peers = 1 + jnp.where(tm > 0, 1, 0) + jnp.where(tm < n_tm - 1, 1, 0)
-    pl.semaphore_wait(barrier, n_mel * rows_of_peers - 1)
 
     halo = []
 
@@ -180,21 +196,6 @@
         )
         halo.append((dt, dm, copy))
         pl.when(has(dt, dm))(copy.start)
-
-    for src, dst, width in zip(inputs, wide, WIDTH):
-        rows, cols = src.shape
-        add_halo(
-            0,
-            1,
-            src.at[:, pl.ds(cols - width, width)],
-            dst.at[pl.ds(0, rows), pl.ds(EDGE - width, width)],
-        )
-        add_halo(
-            0,
-            -1,
-            src.at[:, pl.ds(0, width)],
-            dst.at[pl.ds(0, rows), pl.ds(EDGE + cols, width)],
-        )
 
     def exchange(src, dst, send, recv):
         copies = []
@@ -253,9 +254,6 @@
             else:
                 pl.when(sends)(copy.wait_send)
 
-    spec_out[:, pl.ds(0, spec_real.shape[1])] = spec_real[...].astype(BF16)
-    spec_out[:, pl.ds(spec_real.shape[1], spec_imag.shape[1])] = spec_imag[...].astype(BF16)
-
     for load in loads[:6]:
         load.wait()
     o, c = iota2(TILE, 6 * TILE)
@@ -277,6 +275,14 @@
             pack[end, :, pl.ds(chunk * EDGE, EDGE)] = dot(
                 picks[end], jnp.concatenate(parts, axis=0)
             ).astype(BF16)
+    for load in loads[10:12]:
+        load.wait()
+    per = spec_real.shape[1]
+    spec_out[:, pl.ds(0, per)] = real_v[...].astype(BF16)
+    spec_out[:, pl.ds(per, per)] = imag_v[...].astype(BF16)
+
+    rows_of_peers = 1 + jnp.where(tm > 0, 1, 0) + jnp.where(tm < n_tm - 1, 1, 0)
+    pl.semaphore_wait(barrier, n_mel * rows_of_peers - 1)
     for end, dt in ((1, 1), (0, -1)):
         at = 1 - end
         add_halo(dt, 0, pack.at[end], rows_in.at[at, :, pl.ds(EDGE, length)])
@@ -286,8 +292,24 @@
         add_halo(
             dt, -1, pack.at[end, :, pl.ds(0, EDGE)], rows_in.at[at, :, pl.ds(EDGE + length, EDGE)]
         )
+    for src, dst, width in zip(inputs, wide, WIDTH):
+        rows, cols = src.shape
+        add_halo(
+            0,
+            1,
+            src.at[:, pl.ds(cols - width, width)],
+            dst.at[pl.ds(0, rows), pl.ds(EDGE - width, width)],
+        )
+        add_halo(
+            0,
+            -1,
+            src.at[:, pl.ds(0, width)],
+            dst.at[pl.ds(0, rows), pl.ds(EDGE + cols, width)],
+        )
     spec_copies = exchange(spec_out, spec_in, spec_send, spec_recv)
 
+    for load in loads[6:10]:
+        load.wait()
     w4[...] = jnp.zeros(w4.shape, BF16)
     w3[...] = jnp.zeros(w3.shape, BF16)
     half = LANES // 2
@@ -298,22 +320,22 @@
             for n in range(2):
                 j = n - (k - 1)
                 if abs(j) <= 1:
-                    w4[pl.ds(n * LANES, LANES), lanes] = kernel_four[i, j + 1]
-                    w3[pl.ds(n * LANES, half), lanes] = kernel_three[i, j + 1]
-                    w3[pl.ds(n * LANES + half, half), lanes] = kernel_three[i, j + 1]
+                    w4[pl.ds(n * LANES, LANES), lanes] = k4_v[i, j + 1]
+                    w3[pl.ds(n * LANES, half), lanes] = k3_v[i, j + 1]
+                    w3[pl.ds(n * LANES + half, half), lanes] = k3_v[i, j + 1]
                 for a in range(2):
                     pair = []
                     for b in range(2):
                         j = (2 * n + a) - (2 * (k - 1) + b)
                         pair.append(
-                            kernel_two[i, j + 1].astype(F32) if abs(j) <= 1 else blank
+                            k2_v[i, j + 1].astype(F32) if abs(j) <= 1 else blank
                         )
                     w2[pl.ds(n * LANES + a * half, half), lanes] = jnp.concatenate(
                         pair, axis=1
                     ).astype(BF16)
-    mels = mel_power.shape[1]
+    mels = mel_power.shape[0]
     one = kernel_one[...].astype(F32)
-    one = jnp.concatenate([one, one], axis=1)
+    one = jnp.concatenate([one, one], axis=2)
     m, lane = iota2(mels, LANES)
 
     def band(s, carry):
@@ -321,7 +343,7 @@
         for i in range(3):
             value = jnp.zeros((mels, LANES), F32)
             for j in range(3):
-                value = jnp.where(d == j - 1, one[3 * i + j][None, :], value)
+                value = jnp.where(d == j - 1, one[i, j][None, :], value)
             wb[s, pl.ds(i * mels, mels)] = value.astype(BF16)
         wb[s, pl.ds(3 * mels, mels)] = jnp.zeros((mels, LANES), BF16)
         return carry
@@ -331,6 +353,42 @@
         for s in (1, tiles - 2):
             for i in range(3):
                 g[i, s] = jnp.zeros(g.shape[2:], BF16)
+
+    loud = loudness[...]
+    level = loud / (1.0 + loud * jnp.transpose(power_v[...]))
+    level = jnp.concatenate([level, level], axis=1)
+    lane = lax.broadcasted_iota(jnp.int32, level.shape, 1)
+    gain[...] = jnp.where(lane // mels == lax.rem(mel, 2), level, 0.0)
+    loads[12].wait()
+    filters_b[...] = filters_v[...].astype(BF16)
+
+    def tile_at(s, count=1):
+        return pl.ds(pl.multiple_of(s * LANES, LANES), count * LANES)
+
+    def prepare(s, pairs, fine_at, coarse_at, matrix):
+        rows_at = pl.ds(coarse_at, matrix.shape[0])
+        x = e2[pl.ds(fine_at, matrix.shape[1]), tile_at(s, 2 * pairs)]
+        sums = dot(matrix, jnp.maximum(x, jnp.zeros_like(x)))
+        low = lax.broadcasted_iota(jnp.int32, (matrix.shape[0], LANES), 1) < half
+        for u in range(pairs):
+            want = t1[rows_at, tile_at((s - SIDE) // 2 + SIDE + u)].astype(F32)
+            turned = pltpu.roll(want, half, 1)
+            wants = (jnp.where(low, want, turned), jnp.where(low, turned, want))
+            for n in range(2):
+                at = 2 * u + n
+                block = sums[:, at * LANES : (at + 1) * LANES]
+                pre[s + at, rows_at] = 0.25 * (block + pltpu.roll(block, half, 1) - wants[n])
+
+    r, s_ = iota2(coarse, frames)
+    pool_main = as_bf16(s_ // 2 == r, 0.25)
+    r, s_ = iota2(TILE, TILE)
+    pool_tail = as_bf16(coarser(s_, 0) == r, 0.25)
+
+    def early(q, carry):
+        prepare(SIDE + 8 * q, 4, 0, 0, pool_main)
+        return carry
+
+    lax.fori_loop(0, (tiles - 2 * SIDE) // 8, early, 0)
 
     for dt, dm, copy in halo:
         pl.when(has(-dt, -dm))(copy.wait_recv)
@@ -362,24 +420,31 @@
         g[1, s] = value.astype(BF16)
         g[2, s] = pltpu.roll(value, 1, 0).astype(BF16)
 
-    def tile_at(s, count=1):
-        return pl.ds(pl.multiple_of(s * LANES, LANES), count * LANES)
-
     r, s_ = iota2(coarse_rows, coarse_rows)
     mean_rows = as_bf16(r // 2 == s_ // 2, 0.25)
     r, s_ = iota2(coarse_rows, t2.shape[0])
     spread_two = as_bf16(coarser(r, coarse) == s_)
 
-    def top(p, carry):
-        x = e4[:, tile_at(2 * p, 2)].astype(F32)
-        means = dot(mean_rows, jnp.maximum(x, 0.0).astype(BF16))
-        wanted = dot(spread_two, t2[:, tile_at(p + SIDE // 2)])
-        diff = 0.25 * (means[:, :LANES] + means[:, LANES:] - wanted)
-        for n in range(2):
-            shifted(ga, 2 * p + n, jnp.where(x[:, n * LANES : (n + 1) * LANES] > 0, diff, 0.0))
+    batch = 4
+
+    def top(b, carry):
+        x = e4[:, tile_at(2 * batch * b, 2 * batch)]
+        means = dot(mean_rows, jnp.maximum(x, jnp.zeros_like(x)))
+        wanted = dot(spread_two, t2[:, tile_at(batch * b + SIDE // 2, batch)])
+        for u in range(batch):
+            one_, two = (means[:, (2 * u + n) * LANES : (2 * u + n + 1) * LANES] for n in (0, 1))
+            diff = 0.25 * (one_ + two - wanted[:, u * LANES : (u + 1) * LANES])
+            for n in range(2):
+                at = 2 * u + n
+                mask = x[:, at * LANES : (at + 1) * LANES].astype(F32) > 0
+                shifted(ga, 2 * batch * b + at, jnp.where(mask, diff, 0.0))
         return carry
 
-    lax.fori_loop(0, tiles // 2, top, 0)
+    lax.fori_loop(0, tiles // (2 * batch), top, 0)
+
+    for s in (2, tiles - 4):
+        prepare(s, 1, 0, 0, pool_main)
+    prepare(2, (tiles - 4) // 2, frames, coarse, pool_tail)
 
     def conv(g, weights, group, epilogue):
         rows = g.shape[2]
@@ -411,23 +476,15 @@
 
     conv(ga, w4, 6, third)
 
-    r, s_ = iota2(coarse_rows, fine_rows)
-    pool_rows = as_bf16(coarser(s_, frames) == r, 0.25)
     r, s_ = iota2(fine_rows, coarse_rows)
     spread_rows = as_bf16(coarser(r, frames) == s_)
-    low = lax.broadcasted_iota(jnp.int32, (coarse_rows, LANES), 1) < half
 
     def second(s, value):
         x = e2[:, tile_at(s, 2)].astype(F32)
-        sums = dot(pool_rows, jnp.maximum(x, 0.0).astype(BF16))
-        want = t1[:, tile_at((s - SIDE) // 2 + SIDE)].astype(F32)
-        turned = pltpu.roll(want, half, 1)
-        wants = (jnp.where(low, want, turned), jnp.where(low, turned, want))
         parts = []
         for n in range(2):
             lanes = slice(n * LANES, (n + 1) * LANES)
-            feat = sums[:, lanes] + pltpu.roll(sums[:, lanes], half, 1)
-            parts.append((0.25 * (value[:, lanes] + feat - wants[n])).astype(BF16))
+            parts.append((0.25 * value[:, lanes] + pre[s + n]).astype(BF16))
         fine = dot(spread_rows, jnp.concatenate(parts, axis=1))
         masked = jnp.where(x > 0, fine, 0.0)
         for n in range(2):
@@ -444,34 +501,29 @@
     conv(gc, w2, 3, first)
 
     total = jnp.zeros((fine_rows, 4 * mels), F32)
-    for s in range(2, tiles - 2, 2):
+    span = 12
+    for s in range(2, tiles - 2, span):
         total += dot_nt(
-            jnp.concatenate([gd[s], gd[s + 1]], axis=1),
-            jnp.concatenate([wb[s], wb[s + 1]], axis=1),
+            jnp.concatenate([gd[s + k] for k in range(span)], axis=1),
+            jnp.concatenate([wb[s + k] for k in range(span)], axis=1),
         )
     left, right = total[:, : 2 * mels], total[:, 2 * mels :]
     grad_log = (
         pltpu.roll(left, fine_rows - 1, 0) + pltpu.roll(left, mels, 1) + pltpu.roll(right, 1, 0)
     )[:frames, :mels]
-    loud = loudness[...]
-    grad_mel = grad_log * loud / (1.0 + loud * mel_power[...])
-    twice = jnp.concatenate([grad_mel, grad_mel], axis=1)
-    lane = lax.broadcasted_iota(jnp.int32, twice.shape, 1)
-    mel_out[...] = jnp.where(lane // mels == lax.rem(mel, 2), twice, 0.0).astype(BF16)
+    mel_out[...] = (jnp.concatenate([grad_log, grad_log], axis=1) * gain[...]).astype(BF16)
     mel_copies = exchange(mel_out, mel_in, mel_send, mel_recv)
 
     for dt, dm, copy in halo:
         pl.when(has(dt, dm))(copy.wait_send)
     finish(spec_copies)
-    loads[6].wait()
-    loads[7].wait()
+    loads[13].wait()
     finish(mel_copies)
 
     whole = jnp.concatenate(
         [mel_in[2 * a] + mel_in[2 * a + 1] for a in range(n_mel // 2)], axis=1
     )
-    power = dot_nt(whole, filters_v[...].astype(BF16))
-    per = spec_real.shape[1]
+    power = dot_nt(whole, filters_b[...])
     grads = []
     for part in range(2):
         for j in range(n_mel):
@@ -517,7 +569,7 @@
     result = pl.pallas_call(
         functools.partial(kernel, n_tm, n_mel),
         out_shape=jax.ShapeDtypeStruct((share * bins // LANES, LANES), F32),
-        in_specs=[any_spec] * 8 + [vmem] * 8,
+        in_specs=[any_spec] * 8 + [vmem] + [any_spec] * 4 + [vmem] + [any_spec] * 2,
         out_specs=vmem,
         scratch_shapes=[
             ext(act_one),
@@ -534,6 +586,15 @@
             pltpu.VMEM((3, tiles, coarse_rows, LANES), BF16),
             pltpu.VMEM((3, tiles, fine_rows, LANES), BF16),
             pltpu.VMEM((tiles, fine_rows, LANES), BF16),
+            pltpu.VMEM((tiles, coarse_rows, LANES), F32),
+            pltpu.VMEM((frames, 2 * mels), F32),
+            pltpu.VMEM(filters.shape, BF16),
+            pltpu.VMEM(kernel_two.shape, BF16),
+            pltpu.VMEM(kernel_three.shape, BF16),
+            pltpu.VMEM(kernel_four.shape, BF16),
+            pltpu.VMEM((mels, frames), F32),
+            pltpu.VMEM(spec_real.shape, F32),
+            pltpu.VMEM(spec_imag.shape, F32),
             pltpu.VMEM((2 * LANES, 12 * LANES), BF16),
             pltpu.VMEM((2 * LANES, 12 * LANES), BF16),
             pltpu.VMEM((2 * LANES, 12 * LANES), BF16),
@@ -542,7 +603,7 @@
             pltpu.VMEM((n_mel, share + TILE, 2 * spec_real.shape[1]), BF16),
             pltpu.VMEM((frames, 2 * mels), BF16),
             pltpu.VMEM((n_mel, share + TILE, 2 * mels), BF16),
-            pltpu.SemaphoreType.DMA((8,)),
+            pltpu.SemaphoreType.DMA((14,)),
             pltpu.SemaphoreType.DMA((18,)),
             pltpu.SemaphoreType.DMA((18,)),
             pltpu.SemaphoreType.DMA((2 * n_mel,)),
@@ -563,11 +624,11 @@
         target_two,
         filters,
         table,
-        kernel_one.reshape(9, kernel_one.shape[3]),
+        jnp.transpose(kernel_one, (0, 2, 1, 3)).reshape(3, 3, kernel_one.shape[3]),
         kernel_two,
         kernel_three,
         kernel_four,
-        mel_power,
+        mel_power.T,
         loudness.reshape(1, mels),
         spec_real,
         spec_imag,

time: 39.2 us -> 30.4 us (0.78); the launches traced: 38.5 us -> 30.2 us
  Pallas kernels: 34.3 us -> 28.7 us
  local copies, waits for them, and re-layouts: 4.25 us -> 1.47 us
    pallas_call x1, Pallas kernels: 34.3 us -> 28.7 us  [shards(): pl.pallas_call(functools.partial(kernel, n_tm, n_mel), out_shape=jax.Shap...]
    unnamed x2 -> x1, local copies, waits for them, and re-layouts: 2.96 us -> 1.47 us
    reshape x1 -> x0, local copies, waits for them, and re-layouts: 1.29 us -> none  [shards(): kernel_one.reshape(9, kernel_one.shape[3])]
where the time goes in v1:
time: 30.4 us; the launch traced here: 30.2 us
  Pallas kernels  28.7 us (94%)
  local copies, waits for them, and re-layouts  1.47 us (5%)
    pallas_call x1, Pallas kernels, shards(): pl.pallas_call(functools.partial(kernel, n_tm, n_mel), out_shape=jax.Shap...  28.7 us
    unnamed x1, local copies, waits for them, and re-layouts  1.47 us

profile of v1, /device:TPU:25, one launch (start us, length us, event | category | flops | bytes accessed | tf_op | source)
XLA Modules:
  0.0 30.2 jit_solution(17503945877496564931)
XLA Ops:
  0.0 28.7 %wave_gradient.1 = f32[128,128]{1,0:T(8,128)} custom-call(bf16[128,4096]{1,0:T(8,128)(2,1)} %act_one.1, bf16[128,4096]{1,0:T(8,128)(2,1)} %act_two.1, bf16[64,4096]{1,0:T(8,128)(2,1)} %act_three.1, bf16[64,4096]{1,0:T(8,128)(2,1)} %act_four.1, bf16[64,2048]{1,0:T(8,128)(2,1)} %target_one.1, bf16[32,2048]{1,0:T(8,128)(2,1)} %target_two.1, ...), custom_call_target="tpu_custom_call" | custom-call | tf_op jit(solution)/shard_map/wave_gradient/pallas_call | solution.py:569
  28.7 1.5 %copy.18 = f32[16384]{0:T(1024)} copy(f32[16384]{0:T(1024)} %bitcast.4) | data formatting | bytes 131072

commit v2 on v1

--- a/solution.py
+++ b/solution.py
@@ -20,6 +20,7 @@
 DEPTH = (1, 2, 2, 4, 1, 2)
 PLACE = (0, 1, 3, 5, 9, 10)
 WIDTH = (128, 128, 256, 512, 128, 256)
+GROUPS = ((3, 5), (2, 1, 0, 4))
 
 
 def synthesis_table(bins):
@@ -83,8 +84,10 @@
     t2,
     filters_v,
     table_v,
-    pack,
-    rows_in,
+    pack_out,
+    pack_in,
+    corner_out,
+    corner_in,
     ga,
     gb,
     gc,
@@ -149,7 +152,8 @@
         rows, cols = src.shape
         dst[pl.ds(0, rows), pl.ds(0, EDGE)] = jnp.zeros((rows, EDGE), BF16)
         dst[pl.ds(0, rows), pl.ds(EDGE + cols, EDGE)] = jnp.zeros((rows, EDGE), BF16)
-    rows_in[...] = jnp.zeros(rows_in.shape, BF16)
+    pack_in[...] = jnp.zeros(pack_in.shape, BF16)
+    corner_in[...] = jnp.zeros(corner_in.shape, BF16)
     spec_in[...] = jnp.zeros(spec_in.shape, BF16)
     mel_in[...] = jnp.zeros(mel_in.shape, BF16)
 
@@ -264,17 +268,44 @@
         first_rows |= inside & (c - x * TILE == o - PLACE[x])
         last_rows |= inside & (c - x * TILE - (TILE - DEPTH[x]) == o - PLACE[x])
     picks = (as_bf16(first_rows), as_bf16(last_rows))
-    target_length = target_one.shape[1]
-    for chunk in range(length // EDGE):
+    counts = [src.shape[1] // EDGE for src in inputs]
+
+    def tail_parts(x, end, chunks):
+        src, dst = inputs[x], wide[x]
+        row = src.shape[0] - TILE if end else 0
+        return [dst[pl.ds(row, TILE), pl.ds(EDGE + at * EDGE, EDGE)] for at in chunks]
+
+    def travels(group, end, o, k):
+        found = jnp.zeros(o.shape, jnp.bool_)
+        first = base = 0
+        for x in group:
+            inner = k - first
+            row = inner % TILE - (TILE - DEPTH[x] if end else 0)
+            found |= (
+                (inner >= 0)
+                & (inner < counts[x] * TILE)
+                & (row >= 0)
+                & (row < DEPTH[x])
+                & (o == base + DEPTH[x] * (inner // TILE) + row)
+            )
+            first += counts[x] * TILE
+            base += counts[x] * DEPTH[x]
+        return found
+
+    pack_rows = pack_out.shape[2]
+    for g, group in enumerate(GROUPS):
+        o, k = iota2(pack_rows, sum(counts[x] for x in group) * TILE)
         for end in (0, 1):
-            parts = []
-            for x, (src, dst) in enumerate(zip(inputs, wide)):
-                lane = EDGE + (chunk * EDGE) % (target_length if x >= 4 else length)
-                row = src.shape[0] - TILE if end else 0
-                parts.append(dst[pl.ds(row, TILE), pl.ds(lane, EDGE)])
-            pack[end, :, pl.ds(chunk * EDGE, EDGE)] = dot(
-                picks[end], jnp.concatenate(parts, axis=0)
+            parts = [p for x in group for p in tail_parts(x, end, range(counts[x]))]
+            pack_out[g, end] = dot(
+                as_bf16(travels(group, end, o, k)), jnp.concatenate(parts, axis=0)
             ).astype(BF16)
+    for end in (0, 1):
+        for side in (0, 1):
+            parts = [
+                p for x in range(6) for p in tail_parts(x, end, [counts[x] - 1 if side else 0])
+            ]
+            corner_out[end, side] = dot(picks[end], jnp.concatenate(parts, axis=0)).astype(BF16)
     for load in loads[10:12]:
         load.wait()
     per = spec_real.shape[1]
@@ -283,16 +314,10 @@
 
     rows_of_peers = 1 + jnp.where(tm > 0, 1, 0) + jnp.where(tm < n_tm - 1, 1, 0)
     pl.semaphore_wait(barrier, n_mel * rows_of_peers - 1)
-    for end, dt in ((1, 1), (0, -1)):
-        at = 1 - end
-        add_halo(dt, 0, pack.at[end], rows_in.at[at, :, pl.ds(EDGE, length)])
-        add_halo(
-            dt, 1, pack.at[end, :, pl.ds(length - EDGE, EDGE)], rows_in.at[at, :, pl.ds(0, EDGE)]
-        )
-        add_halo(
-            dt, -1, pack.at[end, :, pl.ds(0, EDGE)], rows_in.at[at, :, pl.ds(EDGE + length, EDGE)]
-        )
-    for src, dst, width in zip(inputs, wide, WIDTH):
+    ends = ((1, 1), (0, -1))
+
+    def lateral(x):
+        src, dst, width = inputs[x], wide[x], WIDTH[x]
         rows, cols = src.shape
         add_halo(
             0,
@@ -306,6 +331,19 @@
             src.at[:, pl.ds(0, width)],
             dst.at[pl.ds(0, rows), pl.ds(EDGE + cols, width)],
         )
+
+    for end, dt in ends:
+        add_halo(dt, 0, pack_out.at[0, end], pack_in.at[0, 1 - end])
+    for x in GROUPS[0]:
+        lateral(x)
+    for end, dt in ends:
+        add_halo(dt, 1, corner_out.at[end, 1], corner_in.at[1 - end, 0])
+        add_halo(dt, -1, corner_out.at[end, 0], corner_in.at[1 - end, 1])
+    needed_first = len(halo)
+    for end, dt in ends:
+        add_halo(dt, 0, pack_out.at[1, end], pack_in.at[1, 1 - end])
+    for x in GROUPS[1]:
+        lateral(x)
     spec_copies = exchange(spec_out, spec_in, spec_send, spec_recv)
 
     for load in loads[6:10]:
@@ -390,8 +428,25 @@
 
     lax.fori_loop(0, (tiles - 2 * SIDE) // 8, early, 0)
 
-    for dt, dm, copy in halo:
-        pl.when(has(-dt, -dm))(copy.wait_recv)
+    def arrive(g):
+        for dt, dm, copy in halo[needed_first:] if g else halo[:needed_first]:
+            pl.when(has(-dt, -dm))(copy.wait_recv)
+        group = GROUPS[g]
+        k, o = iota2(sum(counts[x] for x in group) * TILE, pack_rows)
+        spots = jnp.concatenate(
+            [as_bf16(travels(group, 1, o, k)), as_bf16(travels(group, 0, o, k))], axis=1
+        )
+        both = jnp.concatenate([pack_in[g, 0], pack_in[g, 1]], axis=0)
+        placed = dot(spots, both).astype(BF16)
+        first = 0
+        for x in group:
+            for at in range(counts[x]):
+                wide[x][pl.ds(inputs[x].shape[0], TILE), pl.ds(EDGE + at * EDGE, EDGE)] = placed[
+                    first : first + TILE
+                ]
+                first += TILE
+
+    arrive(0)
     o, c = iota2(6 * TILE, 2 * TILE)
     spots = jnp.zeros((6 * TILE, 2 * TILE), jnp.bool_)
     for x in range(6):
@@ -399,19 +454,11 @@
             r, p = o - x * TILE - base, c - at * TILE - PLACE[x]
             spots |= (r == p) & (r >= 0) & (r < DEPTH[x])
     spots = as_bf16(spots)
-    chunks = (length + 2 * EDGE) // EDGE
-    target_chunks = target_length // EDGE
-    for chunk in range(chunks):
-        lanes = pl.ds(chunk * EDGE, EDGE)
-        both = jnp.concatenate([rows_in[0, :, lanes], rows_in[1, :, lanes]], axis=0)
+    for side in (0, 1):
+        both = jnp.concatenate([corner_in[0, side], corner_in[1, side]], axis=0)
         placed = dot(spots, both).astype(BF16)
         for x, (src, dst) in enumerate(zip(inputs, wide)):
-            at = lanes
-            if x >= 4:
-                if chunk == chunks - 1:
-                    at = pl.ds((target_chunks + 1) * EDGE, EDGE)
-                elif chunk > target_chunks:
-                    continue
+            at = pl.ds((counts[x] + 1) * EDGE if side else 0, EDGE)
             dst[pl.ds(src.shape[0], TILE), at] = placed[x * TILE : (x + 1) * TILE]
 
     def shifted(g, s, value):
@@ -442,6 +489,7 @@
 
     lax.fori_loop(0, tiles // (2 * batch), top, 0)
 
+    arrive(1)
     for s in (2, tiles - 4):
         prepare(s, 1, 0, 0, pool_main)
     prepare(2, (tiles - 4) // 2, frames, coarse, pool_tail)
@@ -564,6 +612,11 @@
     length = act_one.shape[1]
     tiles = (length + 2 * EDGE) // LANES
     fine_rows, coarse_rows = frames + TILE, frames // 2 + TILE
+    arrays = (act_one, act_two, act_three, act_four, target_one, target_two)
+    pack_rows = max(
+        sum(DEPTH[x] * (arrays[x].shape[1] // EDGE) for x in group) for group in GROUPS
+    )
+    pack_rows = -(-pack_rows // TILE) * TILE
     any_spec = pl.BlockSpec(memory_space=pl.ANY)
     vmem = pl.BlockSpec(memory_space=pltpu.VMEM)
     result = pl.pallas_call(
@@ -580,8 +633,10 @@
             ext(target_two),
             pltpu.VMEM(filters.shape, F32),
             pltpu.VMEM(table.shape, BF16),
-            pltpu.VMEM((2, TILE, length), BF16),
-            pltpu.VMEM((2, TILE, length + 2 * EDGE), BF16),
+            pltpu.VMEM((2, 2, pack_rows, EDGE), BF16),
+            pltpu.VMEM((2, 2, pack_rows, EDGE), BF16),
+            pltpu.VMEM((2, 2, TILE, EDGE), BF16),
+            pltpu.VMEM((2, 2, TILE, EDGE), BF16),
             pltpu.VMEM((3, tiles, coarse_rows, LANES), BF16),
             pltpu.VMEM((3, tiles, coarse_rows, LANES), BF16),
             pltpu.VMEM((3, tiles, fine_rows, LANES), BF16),
@@ -604,8 +659,8 @@
             pltpu.VMEM((frames, 2 * mels), BF16),
             pltpu.VMEM((n_mel, share + TILE, 2 * mels), BF16),
             pltpu.SemaphoreType.DMA((14,)),
-            pltpu.SemaphoreType.DMA((18,)),
-            pltpu.SemaphoreType.DMA((18,)),
+            pltpu.SemaphoreType.DMA((20,)),
+            pltpu.SemaphoreType.DMA((20,)),
             pltpu.SemaphoreType.DMA((2 * n_mel,)),
             pltpu.SemaphoreType.DMA((2 * n_mel,)),
             pltpu.SemaphoreType.DMA((2 * n_mel,)),

time: 30.4 us -> 28.3 us (0.931)
  Pallas kernels: 28.7 us -> 26.6 us
    pallas_call x1, Pallas kernels: 28.7 us -> 26.6 us  [shards(): pl.pallas_call(functools.partial(kernel, n_tm, n_mel), out_shape=jax.Shap...]
where the time goes in v2:
time: 28.3 us; the launch traced here: 28.1 us
  Pallas kernels  26.6 us (94%)
  local copies, waits for them, and re-layouts  1.47 us (5%)
    pallas_call x1, Pallas kernels, shards(): pl.pallas_call(functools.partial(kernel, n_tm, n_mel), out_shape=jax.Shap...  26.6 us
    unnamed x1, local copies, waits for them, and re-layouts  1.47 us

profile of v2, /device:TPU:25, one launch (start us, length us, event | category | flops | bytes accessed | tf_op | source)
XLA Modules:
  0.0 28.1 jit_solution(12794116284090995072)
XLA Ops:
  0.0 26.6 %wave_gradient.1 = f32[128,128]{1,0:T(8,128)} custom-call(bf16[128,4096]{1,0:T(8,128)(2,1)} %act_one.1, bf16[128,4096]{1,0:T(8,128)(2,1)} %act_two.1, bf16[64,4096]{1,0:T(8,128)(2,1)} %act_three.1, bf16[64,4096]{1,0:T(8,128)(2,1)} %act_four.1, bf16[64,2048]{1,0:T(8,128)(2,1)} %target_one.1, bf16[32,2048]{1,0:T(8,128)(2,1)} %target_two.1, ...), custom_call_target="tpu_custom_call" | custom-call | tf_op jit(solution)/shard_map/wave_gradient/pallas_call | solution.py:622
  26.6 1.5 %copy.18 = f32[16384]{0:T(1024)} copy(f32[16384]{0:T(1024)} %bitcast.4) | data formatting | bytes 131072

commit v3 on v2

--- a/solution.py
+++ b/solution.py
@@ -104,6 +104,7 @@
     w4,
     w3,
     w2,
+    band,
     wb,
     spec_out,
     spec_in,
@@ -374,19 +375,19 @@
     mels = mel_power.shape[0]
     one = kernel_one[...].astype(F32)
     one = jnp.concatenate([one, one], axis=2)
-    m, lane = iota2(mels, LANES)
-
-    def band(s, carry):
-        d = m - (2 * (s - SIDE) + lane // half)
+    reach = 2 * (tiles - SIDE)
+    row, lane = iota2(band.shape[1], LANES)
+    d = row - reach - lane // half
+    for i in range(3):
+        value = jnp.zeros(d.shape, F32)
+        for j in range(3):
+            value = jnp.where(d == j - 1, one[i, j][None, :], value)
+        band[i] = value
+    for s in range(2, tiles - 2):
         for i in range(3):
-            value = jnp.zeros((mels, LANES), F32)
-            for j in range(3):
-                value = jnp.where(d == j - 1, one[i, j][None, :], value)
-            wb[s, pl.ds(i * mels, mels)] = value.astype(BF16)
+            at = reach - 2 * (s - SIDE)
+            wb[s, pl.ds(i * mels, mels)] = band[i, pl.ds(at, mels)].astype(BF16)
         wb[s, pl.ds(3 * mels, mels)] = jnp.zeros((mels, LANES), BF16)
-        return carry
-
-    lax.fori_loop(2, tiles - 2, band, 0)
     for g in (gb, gc):
         for s in (1, tiles - 2):
             for i in range(3):
@@ -397,8 +398,6 @@
     level = jnp.concatenate([level, level], axis=1)
     lane = lax.broadcasted_iota(jnp.int32, level.shape, 1)
     gain[...] = jnp.where(lane // mels == lax.rem(mel, 2), level, 0.0)
-    loads[12].wait()
-    filters_b[...] = filters_v[...].astype(BF16)
 
     def tile_at(s, count=1):
         return pl.ds(pl.multiple_of(s * LANES, LANES), count * LANES)
@@ -426,7 +425,8 @@
         prepare(SIDE + 8 * q, 4, 0, 0, pool_main)
         return carry
 
-    lax.fori_loop(0, (tiles - 2 * SIDE) // 8, early, 0)
+    for q in range((tiles - 2 * SIDE) // 8):
+        early(q, 0)
 
     def arrive(g):
         for dt, dm, copy in halo[needed_first:] if g else halo[:needed_first]:
@@ -487,7 +487,8 @@
                 shifted(ga, 2 * batch * b + at, jnp.where(mask, diff, 0.0))
         return carry
 
-    lax.fori_loop(0, tiles // (2 * batch), top, 0)
+    for b in range(tiles // (2 * batch)):
+        top(b, 0)
 
     arrive(1)
     for s in (2, tiles - 4):
@@ -514,7 +515,8 @@
                 epilogue(base + 2 * u, result[u * rows : (u + 1) * rows])
             return carry
 
-        lax.fori_loop(0, pairs // group, step, 0)
+        for q in range(pairs // group):
+            step(q, 0)
 
     def third(s, value):
         x = e3[:, tile_at(s, 2)].astype(F32)
@@ -564,6 +566,8 @@
 
     for dt, dm, copy in halo:
         pl.when(has(dt, dm))(copy.wait_send)
+    loads[12].wait()
+    filters_b[...] = filters_v[...].astype(BF16)
     finish(spec_copies)
     loads[13].wait()
     finish(mel_copies)
@@ -653,6 +657,7 @@
             pltpu.VMEM((2 * LANES, 12 * LANES), BF16),
             pltpu.VMEM((2 * LANES, 12 * LANES), BF16),
             pltpu.VMEM((2 * LANES, 12 * LANES), BF16),
+            pltpu.VMEM((3, 2 * (tiles + SIDE) + mels, LANES), F32),
             pltpu.VMEM((tiles, 4 * mels, LANES), BF16),
             pltpu.VMEM((frames, 2 * spec_real.shape[1]), BF16),
             pltpu.VMEM((n_mel, share + TILE, 2 * spec_real.shape[1]), BF16),

time: 28.3 us -> 25.7 us (0.908)
  Pallas kernels: 26.6 us -> 24 us
    pallas_call x1, Pallas kernels: 26.6 us -> 24 us  [shards(): pl.pallas_call(functools.partial(kernel, n_tm, n_mel), out_shape=jax.Shap...]
where the time goes in v3:
time: 25.7 us; the launch traced here: 25.5 us
  Pallas kernels  24 us (93%)
  local copies, waits for them, and re-layouts  1.47 us (6%)
    pallas_call x1, Pallas kernels, shards(): pl.pallas_call(functools.partial(kernel, n_tm, n_mel), out_shape=jax.Shap...  24 us
    unnamed x1, local copies, waits for them, and re-layouts  1.47 us

profile of v3, /device:TPU:25, one launch (start us, length us, event | category | flops | bytes accessed | tf_op | source)
XLA Modules:
  0.0 25.5 jit_solution(8761384365078313815)
XLA Ops:
  0.0 24.0 %wave_gradient.1 = f32[128,128]{1,0:T(8,128)} custom-call(bf16[128,4096]{1,0:T(8,128)(2,1)} %act_one.1, bf16[128,4096]{1,0:T(8,128)(2,1)} %act_two.1, bf16[64,4096]{1,0:T(8,128)(2,1)} %act_three.1, bf16[64,4096]{1,0:T(8,128)(2,1)} %act_four.1, bf16[64,2048]{1,0:T(8,128)(2,1)} %target_one.1, bf16[32,2048]{1,0:T(8,128)(2,1)} %target_two.1, ...), custom_call_target="tpu_custom_call" | custom-call | tf_op jit(solution)/shard_map/wave_gradient/pallas_call | solution.py:626
  24.0 1.5 %copy.18 = f32[16384]{0:T(1024)} copy(f32[16384]{0:T(1024)} %bitcast.4) | data formatting | bytes 131072

commit v4 on v3

--- a/solution.py
+++ b/solution.py
@@ -24,13 +24,21 @@
 
 
 def synthesis_table(bins):
+    points, hop = 2 * bins, bins
+    bin_at = np.concatenate([np.arange(0, bins, 2), np.arange(1, bins, 2)])
+    angle = (bin_at[:, None] * np.arange(hop)[None, :] % points) * (2.0 * np.pi / points)
+    scale = 2.0 * points**-0.5
+    half = bins // 2
+    parts = []
+    for at in (slice(0, half), slice(half, bins)):
+        parts += [np.cos(angle[at]) * scale, -np.sin(angle[at]) * scale]
+    return np.concatenate(parts, axis=0).astype(np.float32).astype(ml_dtypes.bfloat16)
+
+
+def hann_halves(bins):
     points = 2 * bins
-    sample = np.arange(points)
-    angle = (np.arange(bins)[:, None] * sample[None, :] % points) * (2.0 * np.pi / points)
-    window = 0.5 - 0.5 * np.cos(sample * (2.0 * np.pi / points))
-    scale = 2.0 * window * points**-0.5
-    table = np.concatenate([np.cos(angle) * scale, -np.sin(angle) * scale], axis=0)
-    return table.astype(np.float32).astype(ml_dtypes.bfloat16)
+    window = 0.5 - 0.5 * np.cos(np.arange(points) * (2.0 * np.pi / points))
+    return window.reshape(2, bins).astype(np.float32)
 
 
 def iota2(rows, cols):
@@ -75,6 +83,7 @@
     loudness,
     spec_real,
     spec_imag,
+    window,
     out,
     e1,
     e2,
@@ -142,7 +151,8 @@
         (mel_power, power_v),
         (spec_real, real_v),
         (spec_imag, imag_v),
-        (filters, filters_v),
+        (filters.at[:, pl.ds(0, LANES)], filters_v.at[0]),
+        (filters.at[:, pl.ds(LANES, LANES)], filters_v.at[1]),
         (table, table_v),
     ):
         loads.append(pltpu.make_async_copy(src, dst, load_sem.at[len(loads)]))
@@ -310,8 +320,10 @@
     for load in loads[10:12]:
         load.wait()
     per = spec_real.shape[1]
-    spec_out[:, pl.ds(0, per)] = real_v[...].astype(BF16)
-    spec_out[:, pl.ds(per, per)] = imag_v[...].astype(BF16)
+    k, c = iota2(per, per)
+    even_first = as_bf16(k == jnp.where(c < per // 2, 2 * c, 2 * c - per + 1))
+    spec_out[:, pl.ds(0, per)] = dot(real_v[...].astype(BF16), even_first).astype(BF16)
+    spec_out[:, pl.ds(per, per)] = dot(imag_v[...].astype(BF16), even_first).astype(BF16)
 
     rows_of_peers = 1 + jnp.where(tm > 0, 1, 0) + jnp.where(tm < n_tm - 1, 1, 0)
     pl.semaphore_wait(barrier, n_mel * rows_of_peers - 1)
@@ -567,23 +579,41 @@
     for dt, dm, copy in halo:
         pl.when(has(dt, dm))(copy.wait_send)
     loads[12].wait()
-    filters_b[...] = filters_v[...].astype(BF16)
+    loads[13].wait()
+    bins = filters.shape[0]
+    for a in range(2):
+        for odd in (0, 1):
+            filters_b[pl.ds(odd * (bins // 2), bins // 2), pl.ds(a * LANES, LANES)] = filters_v[
+                a, pl.ds(odd, bins // 2, stride=2), :
+            ].astype(BF16)
     finish(spec_copies)
-    loads[13].wait()
+    low = lax.broadcasted_iota(jnp.int32, (spec_in.shape[1], per), 1) < per // 2
+    specs = ([], [])
+    for part in range(2):
+        for a in range(n_mel // 2):
+            one_, two = (
+                spec_in[2 * a + b, :, pl.ds(part * per, per)].astype(F32) for b in (0, 1)
+            )
+            specs[0].append(jnp.where(low, one_, pltpu.roll(two, per // 2, 1)))
+            specs[1].append(jnp.where(low, pltpu.roll(one_, per // 2, 1), two))
+    specs = [jnp.concatenate(parts, axis=1) for parts in specs]
+    loads[14].wait()
     finish(mel_copies)
 
     whole = jnp.concatenate(
         [mel_in[2 * a] + mel_in[2 * a + 1] for a in range(n_mel // 2)], axis=1
     )
     power = dot_nt(whole, filters_b[...])
-    grads = []
-    for part in range(2):
-        for j in range(n_mel):
-            spec = spec_in[j, :, pl.ds(part * per, per)].astype(F32)
-            grads.append((power[:, j * per : (j + 1) * per] * spec).astype(BF16))
-    made = dot(jnp.concatenate(grads, axis=1), table_v[...])
-    hop = made.shape[1] // 2
-    blocks = made[:, :hop] + pltpu.roll(made[:, hop:], 1, 0)
+    made = []
+    for odd in (0, 1):
+        level = power[:, odd * (bins // 2) : (odd + 1) * (bins // 2)]
+        grads = (jnp.concatenate([level, level], axis=1) * specs[odd]).astype(BF16)
+        made.append(dot(grads, table_v[pl.ds(odd * bins, bins), :]))
+    hop = made[0].shape[1]
+    halves = window[...]
+    blocks = (made[0] + made[1]) * halves[0:1] + pltpu.roll(
+        (made[0] - made[1]) * halves[1:2], 1, 0
+    )
     for a in range(hop // LANES):
         out[pl.ds(a, share, stride=hop // LANES), :] = blocks[
             :share, a * LANES : (a + 1) * LANES
@@ -626,7 +656,7 @@
     result = pl.pallas_call(
         functools.partial(kernel, n_tm, n_mel),
         out_shape=jax.ShapeDtypeStruct((share * bins // LANES, LANES), F32),
-        in_specs=[any_spec] * 8 + [vmem] + [any_spec] * 4 + [vmem] + [any_spec] * 2,
+        in_specs=[any_spec] * 8 + [vmem] + [any_spec] * 4 + [vmem] + [any_spec] * 2 + [vmem],
         out_specs=vmem,
         scratch_shapes=[
             ext(act_one),
@@ -635,7 +665,7 @@
             ext(act_four),
             ext(target_one),
             ext(target_two),
-            pltpu.VMEM(filters.shape, F32),
+            pltpu.VMEM((2, bins, LANES), F32),
             pltpu.VMEM(table.shape, BF16),
             pltpu.VMEM((2, 2, pack_rows, EDGE), BF16),
             pltpu.VMEM((2, 2, pack_rows, EDGE), BF16),
@@ -663,7 +693,7 @@
             pltpu.VMEM((n_mel, share + TILE, 2 * spec_real.shape[1]), BF16),
             pltpu.VMEM((frames, 2 * mels), BF16),
             pltpu.VMEM((n_mel, share + TILE, 2 * mels), BF16),
-            pltpu.SemaphoreType.DMA((14,)),
+            pltpu.SemaphoreType.DMA((15,)),
             pltpu.SemaphoreType.DMA((20,)),
             pltpu.SemaphoreType.DMA((20,)),
             pltpu.SemaphoreType.DMA((2 * n_mel,)),
@@ -692,6 +722,7 @@
         loudness.reshape(1, mels),
         spec_real,
         spec_imag,
+        jnp.asarray(hann_halves(bins)),
     )
     return result.reshape(-1)
 

time: 25.7 us -> 25.6 us (level)
  no operation moved by 1% of the time
where the time goes in v4:
time: 25.6 us; the launch traced here: 25.4 us
  Pallas kernels  24 us (94%)
  local copies, waits for them, and re-layouts  1.47 us (6%)
    pallas_call x1, Pallas kernels, shards(): pl.pallas_call(functools.partial(kernel, n_tm, n_mel), out_shape=jax.Shap...  24 us
    unnamed x1, local copies, waits for them, and re-layouts  1.47 us

profile of v4, /device:TPU:25, one launch (start us, length us, event | category | flops | bytes accessed | tf_op | source)
XLA Modules:
  0.0 25.4 jit_solution(10270192431988728196)
XLA Ops:
  0.0 24.0 %wave_gradient.1 = f32[128,128]{1,0:T(8,128)} custom-call(bf16[128,4096]{1,0:T(8,128)(2,1)} %act_one.1, bf16[128,4096]{1,0:T(8,128)(2,1)} %act_two.1, bf16[64,4096]{1,0:T(8,128)(2,1)} %act_three.1, bf16[64,4096]{1,0:T(8,128)(2,1)} %act_four.1, bf16[64,2048]{1,0:T(8,128)(2,1)} %target_one.1, bf16[32,2048]{1,0:T(8,128)(2,1)} %target_two.1, ...), custom_call_target="tpu_custom_call" | custom-call | tf_op jit(solution)/shard_map/wave_gradient/pallas_call | solution.py:656
  24.0 1.5 %copy.19 = f32[16384]{0:T(1024)} copy(f32[16384]{0:T(1024)} %bitcast.4) | data formatting | bytes 131072

commit v5 on v4

--- a/solution.py
+++ b/solution.py
@@ -560,7 +560,7 @@
         for n in range(2):
             gd[s + n] = masked[:, n * LANES : (n + 1) * LANES]
 
-    conv(gc, w2, 3, first)
+    conv(gc, w2, 6, first)
 
     total = jnp.zeros((fine_rows, 4 * mels), F32)
     span = 12

time: 25.6 us -> 25.1 us (0.980)
  Pallas kernels: 24 us -> 23.5 us
    pallas_call x1, Pallas kernels: 24 us -> 23.5 us  [shards(): pl.pallas_call(functools.partial(kernel, n_tm, n_mel), out_shape=jax.Shap...]
where the time goes in v5:
time: 25.1 us; the launch traced here: 24.9 us
  Pallas kernels  23.5 us (94%)
  local copies, waits for them, and re-layouts  1.47 us (6%)
    pallas_call x1, Pallas kernels, shards(): pl.pallas_call(functools.partial(kernel, n_tm, n_mel), out_shape=jax.Shap...  23.5 us
    unnamed x1, local copies, waits for them, and re-layouts  1.47 us

profile of v5, /device:TPU:25, one launch (start us, length us, event | category | flops | bytes accessed | tf_op | source)
XLA Modules:
  0.0 24.9 jit_solution(8697345976617197791)
XLA Ops:
  0.0 23.5 %wave_gradient.1 = f32[128,128]{1,0:T(8,128)} custom-call(bf16[128,4096]{1,0:T(8,128)(2,1)} %act_one.1, bf16[128,4096]{1,0:T(8,128)(2,1)} %act_two.1, bf16[64,4096]{1,0:T(8,128)(2,1)} %act_three.1, bf16[64,4096]{1,0:T(8,128)(2,1)} %act_four.1, bf16[64,2048]{1,0:T(8,128)(2,1)} %target_one.1, bf16[32,2048]{1,0:T(8,128)(2,1)} %target_two.1, ...), custom_call_target="tpu_custom_call" | custom-call | tf_op jit(solution)/shard_map/wave_gradient/pallas_call | solution.py:656
  23.5 1.5 %copy.19 = f32[16384]{0:T(1024)} copy(f32[16384]{0:T(1024)} %bitcast.4) | data formatting | bytes 131072
